TPU v7x, 512 devices: a whole 4x4x16 slice. The times are simulated.
512 devices in a mesh: tm: 32 (over z, core), panel: 16 (over y, x).
Axes of the slice: x: 4, y: 4, z: 16, core: 2. Of those that a mesh axis runs over, the one named last changes fastest.
Arguments:
- kept_block: float32 [32, 1024, 1024], P('tm', 'panel'), may hold values from -6 to 6
- coupling_in: bfloat16 [32, 1024, 1024], P('tm', None, 'panel'), may hold values from -0.375 to 0.375
- coupling_out: bfloat16 [32, 1024, 1024], P('tm', 'panel'), may hold values from -0.375 to 0.375
- factor: bfloat16 [32, 1024, 1024], P('tm', 'panel'), may hold values from -0.1875 to 0.1875
- source_kept: bfloat16 [32, 1024, 1024], P('tm', 'panel'), may hold values from -6 to 6
- source_odd: bfloat16 [32, 1024, 1024], P('tm', 'panel'), may hold values from -6 to 6
- observed: int32 [32, 1024], P('tm', 'panel'), may hold values 0 or 1
Outputs:
- reduced_block: float32 [32, 1024, 1024], P('tm', 'panel')
- reduced_coupling: float32 [32, 1024, 1024], P('tm', 'panel')
- reduced_source: float32 [32, 1024, 1024], P('tm', 'panel')
All inputs are finite; a program needn't handle non-finite values. No bound on the sum of `observed` on one device may be relied on, other than what follows from the above.
Results may differ from a plain program's by a relative error of at most 0.0029.
Values may be sent and summed in bfloat16 or wider, within the bound.
A program may use at most 64 MiB of HBM per device.

v0:
```python
import jax
import jax.numpy as jnp
from jax import lax
from jax.sharding import PartitionSpec as P

obs_precision = 2.0


def shifted(value, axis, by):
    length = lax.axis_size(axis)
    pairs = [(i, i + by) for i in range(length) if 0 <= i + by < length]
    return lax.ppermute(value, axis, pairs)


def cross_product(left, right):
    return lax.dot_general(
        left, right, (((0,), (0,)), ((), ())), preferred_element_type=jnp.float32
    )


def body(kept_block, coupling_in, coupling_out, factor, source_kept, source_odd, observed):
    panel_rows = kept_block.shape[1]
    nodes = kept_block.shape[2]
    couple_in = coupling_in[0]
    couple_out = coupling_out[0]
    odd_full = lax.all_gather(source_odd[0], "panel", axis=0, tiled=True)
    piece = lax.all_gather(factor[0], "panel", axis=0, tiled=True)
    first = jnp.dot(piece, couple_in, preferred_element_type=jnp.float32).astype(jnp.bfloat16)
    second = lax.dot_general(
        piece, couple_out, (((1,), (1,)), ((), ())), preferred_element_type=jnp.float32
    ).astype(jnp.bfloat16)
    third = jnp.dot(piece, odd_full, preferred_element_type=jnp.float32).astype(jnp.bfloat16)
    stacked = jnp.concatenate([first, second, third], axis=1)
    whitened_in = stacked[:, :panel_rows]
    whitened_out = stacked[:, panel_rows : 2 * panel_rows]
    whitened_src = stacked[:, 2 * panel_rows :]
    partner, partner_src = shifted((whitened_out, whitened_src), "tm", 1)
    partner_all, whitened_all = (
        lax.all_gather(partner, "panel", axis=1, tiled=True),
        lax.all_gather(whitened_in, "panel", axis=1, tiled=True),
    )
    row_index = lax.axis_index("panel") * panel_rows + lax.broadcasted_iota(
        jnp.int32, (panel_rows, nodes), 0
    )
    col_index = lax.broadcasted_iota(jnp.int32, (panel_rows, nodes), 1)
    mask_rows = observed[0].astype(jnp.float32)[:, None]
    diagonal = jnp.where(row_index == col_index, mask_rows, jnp.float32(0.0))
    new_block = kept_block[0] + obs_precision * diagonal
    new_block = (
        new_block - cross_product(partner, partner_all) - cross_product(whitened_in, whitened_all)
    )
    new_coupling = -cross_product(whitened_out, whitened_all)
    new_source = source_kept[0].astype(jnp.float32) - cross_product(partner, partner_src)
    new_source = new_source - cross_product(whitened_in, whitened_src)
    return (new_block[None], new_coupling[None], new_source[None])


def solution(mesh):
    return jax.shard_map(
        body,
        mesh=mesh,
        in_specs=(
            P("tm", "panel", None),
            P("tm", None, "panel"),
            P("tm", "panel", None),
            P("tm", "panel", None),
            P("tm", "panel", None),
            P("tm", "panel", None),
            P("tm", "panel"),
        ),
        out_specs=(P("tm", "panel", None), P("tm", "panel", None), P("tm", "panel", None)),
        check_vma=False,
    )
```

profile of v0, /device:TPU:1, one launch (start us, length us, event | category | flops | bytes accessed | tf_op | source)
XLA Modules:
  0.0 274.6 jit_solution(2775091244614220873)
XLA Ops:
  7.2 0.0 copy-start
  7.2 0.0 copy-start.7
  7.2 0.0 all-gather.11.cloned.1.call-start
  7.2 0.7 all-gather.11.cloned.1.call-update
  7.9 0.0 all-gather.13.cloned.1.call-start
  8.0 0.7 all-gather.13.cloned.1.call-update
  8.7 0.0 all-gather.9.cloned.1.call-start
  8.7 67.1 %all-gather.11.cloned.1.call-done = bf16[1,1024,1024]{2,1,0:T(8,128)(2,1)} async-done(((bf16[1,64,1024]{2,1,0:T(8,128)(2,1)}), bf16[1,1024,1024]{2,1,0:T(8,128)(2,1)}) %all-gather.11.cloned.1.call-update) | async-done | bytes 2097168 | tf_op jit(solution)/shard_map/all_gather | solution.py:27
  75.8 0.0 copy-done
  75.8 3.2 %fusion.20 = bf16[1024,64]{0,1:T(8,128)(2,1)} fusion(bf16[1,1024,1024]{2,1,0:T(8,128)(2,1)} %all-gather.11.cloned.1.call-done, bf16[1,1024,64]{1,2,0:T(8,128)(2,1)S(1)} %copy-done), kind=kOutput, calls=%fused_computation.17 | convolution fusion | flops 134283264 | bytes 2359296 | tf_op jit(solution)/shard_map/dot_general | solution.py:28
  78.9 0.0 all-gather.9.cloned.1.call-update
  79.0 0.0 all-gather.7.cloned.1.call-start
  79.0 0.0 copy-done.7
  79.0 0.8 fusion.17
  79.8 4.6 %collective-permute-start = (bf16[1024,64]{0,1:T(8,128)(2,1)S(1)}, bf16[1024,64]{0,1:T(8,128)(2,1)S(1)}, u32[]{:S(2)}, u32[]{:S(2)}) collective-permute-start(bf16[1024,64]{0,1:T(8,128)(2,1)S(1)} %fusion.17), channel_id=1, source_target_pairs={{0,16},{16,32},{32,48},{48,64},{64,80},{80,96},{96,112},{112,128},... | collective-permute-start | bytes 393224 | tf_op jit(solution)/shard_map/ppermute | solution.py:12
  84.4 1.9 collective-permute-done
  86.3 0.7 copy-done.4
  87.0 0.0 all-gather.7.cloned.1.call-update
  87.0 0.0 copy-start.9
  87.0 0.0 copy-start.3
  87.0 51.5 %all-gather.13.cloned.1.call-done = bf16[1,1024,1024]{2,1,0:T(8,128)(2,1)} async-done(((bf16[1,64,1024]{2,1,0:T(8,128)(2,1)}), bf16[1,1024,1024]{2,1,0:T(8,128)(2,1)}) %all-gather.13.cloned.1.call-update) | async-done | bytes 2097168 | tf_op jit(solution)/shard_map/all_gather | solution.py:26
  138.5 5.3 %fusion.7 = bf16[1024,1024]{1,0:T(8,128)(2,1)} fusion(bf16[1,1024,1024]{2,1,0:T(8,128)(2,1)} %all-gather.13.cloned.1.call-done, bf16[1,1024,1024]{2,1,0:T(8,128)(2,1)S(1)} %copy-done.2), kind=kOutput, calls=%fused_computation.7 | convolution fusion | flops 2148532224 | bytes 6291456 | tf_op jit(solution)/shard_map/dot_general | solution.py:32
  143.8 4.7 %collective-permute-start.1 = (bf16[1024,1024]{1,0:T(8,128)(2,1)}, bf16[1024,1024]{1,0:T(8,128)(2,1)S(1)}, u32[]{:S(2)}, u32[]{:S(2)}) collective-permute-start(bf16[1024,1024]{1,0:T(8,128)(2,1)} %fusion.7), channel_id=1, source_target_pairs={{0,16},{16,32},{32,48},{48,64},{64,80},{80,96},{96,112},{112,128},... | collective-permute-start | bytes 6291464 | tf_op jit(solution)/shard_map/ppermute | solution.py:12
  148.5 0.0 copy-done.9
  148.6 2.1 fusion.26
  150.7 21.2 %collective-permute-done.1 = bf16[1024,1024]{1,0:T(8,128)(2,1)S(1)} collective-permute-done((bf16[1024,1024]{1,0:T(8,128)(2,1)}, bf16[1024,1024]{1,0:T(8,128)(2,1)S(1)}, u32[]{:S(2)}, u32[]{:S(2)}) %collective-permute-start.1) | collective-permute-done | bytes 2097184 | tf_op jit(solution)/shard_map/ppermute | solution.py:12
  171.8 1.2 fusion.13
  173.0 28.9 %all-gather.9.cloned.1.call-done = bf16[1024,1024]{0,1:T(8,128)(2,1)} async-done(((bf16[1024,64]{0,1:T(8,128)(2,1)}), bf16[1024,1024]{0,1:T(8,128)(2,1)}) %all-gather.9.cloned.1.call-update) | async-done | bytes 2097168 | tf_op jit(solution)/shard_map/all_gather | solution.py:40
  201.9 3.2 %fusion.16 = f32[1,64,1024]{2,1,0:T(8,128)} fusion(bf16[1024,64]{0,1:T(8,128)(2,1)S(1)} %fusion.17, bf16[1024,1024]{0,1:T(8,128)(2,1)} %all-gather.9.cloned.1.call-done), kind=kOutput, calls=%fused_computation.15 | convolution fusion | flops 134283264 | bytes 2490368 | tf_op jit(solution)/shard_map/dot_general | solution.py:16
  205.1 0.8 fusion.25
  205.8 59.2 %all-gather.7.cloned.1.call-done = bf16[1024,1024]{0,1:T(8,128)(2,1)} async-done(((bf16[1024,64]{0,1:T(8,128)(2,1)}), bf16[1024,1024]{0,1:T(8,128)(2,1)}) %all-gather.7.cloned.1.call-update) | async-done | bytes 2097168 | tf_op jit(solution)/shard_map/all_gather | solution.py:39
  265.0 3.1 %fusion.15 = f32[1,64,1024]{2,1,0:T(8,128)} fusion(f32[64,1024]{1,0:T(8,128)S(1)} %fusion.25, bf16[1024,64]{0,1:T(8,128)(2,1)S(1)} %copy-done.5, bf16[1024,1024]{0,1:T(8,128)(2,1)} %all-gather.7.cloned.1.call-done, f32[1,64,1024]{2,1,0:T(8,128)S(1)} %copy-done.6, f32[64]{0:T(128)S(1)} %convert_bitcast_fusion, s32[64]{0:T(128)S(1)} %iota_add_fusion), kind=kOutput, calls=%fused_computation.13 | convolution fusion | flops 134610944 | bytes 3015168 | tf_op jit(solution)/shard_map/dot_general | solution.py:16
  (14 shorter events, 0.0 us)
Async XLA Ops:
  7.2 68.6 %copy-start = (bf16[1,1024,64]{1,2,0:T(8,128)(2,1)S(1)}, bf16[1,1024,64]{1,2,0:T(8,128)(2,1)}, u32[]{:S(2)}) copy-start(bf16[1,1024,64]{1,2,0:T(8,128)(2,1)} %param.8) | copy-start | bytes 393220
  7.2 71.8 %copy-start.7 = (bf16[1,64,1024]{2,1,0:T(8,128)(2,1)S(1)}, bf16[1,64,1024]{2,1,0:T(8,128)(2,1)}, u32[]{:S(2)}) copy-start(bf16[1,64,1024]{2,1,0:T(8,128)(2,1)} %param.9) | copy-start | bytes 393220
  7.2 68.6 %all-gather.11.cloned.1.call-start = ((), (), s32[]{:S(2)}) async-start(), calls=%async_computation.2 | async-start | bytes 2228224 | tf_op jit(solution)/shard_map/all_gather | solution.py:27
  7.9 130.6 %all-gather.13.cloned.1.call-start = ((), (), s32[]{:S(2)}) async-start(), calls=%async_computation.3 | async-start | bytes 2228224 | tf_op jit(solution)/shard_map/all_gather | solution.py:26
  8.7 193.2 %all-gather.9.cloned.1.call-start = ((), (), s32[]{:S(2)}) async-start(), calls=%async_computation.1 | async-start | bytes 2228224 | tf_op jit(solution)/shard_map/all_gather | solution.py:40
  75.8 3.2 %copy-start.2 = (bf16[1,1024,1024]{2,1,0:T(8,128)(2,1)S(1)}, bf16[1,1024,1024]{2,1,0:T(8,128)(2,1)}, u32[]{:S(2)}) copy-start(bf16[1,1024,1024]{2,1,0:T(8,128)(2,1)} %all-gather.11.cloned.1.call-done) | copy-start | bytes 6291460
  79.0 186.1 %all-gather.7.cloned.1.call-start = ((), (), s32[]{:S(2)}) async-start(), calls=%async_computation | async-start | bytes 2228224 | tf_op jit(solution)/shard_map/all_gather | solution.py:39
  79.8 6.5 %collective-permute-start = (bf16[1024,64]{0,1:T(8,128)(2,1)S(1)}, bf16[1024,64]{0,1:T(8,128)(2,1)S(1)}, u32[]{:S(2)}, u32[]{:S(2)}) collective-permute-start(bf16[1024,64]{0,1:T(8,128)(2,1)S(1)} %fusion.17), channel_id=1, source_target_pairs={{0,16},{16,32},{32,48},{48,64},{64,80},{80,96},{96,112},{112,128},... | collective-permute-start | bytes 393224 | tf_op jit(solution)/shard_map/ppermute | solution.py:12
  86.3 0.7 copy-start.4
  87.0 61.6 %copy-start.9 = (s32[1,64]{1,0:T(1,128)S(1)}, s32[1,64]{1,0:T(1,128)}, u32[]{:S(2)}) copy-start(s32[1,64]{1,0:T(1,128)} %param.13) | copy-start | bytes 772
  87.0 61.6 %copy-start.3 = (bf16[1024,64]{0,1:T(8,128)(2,1)S(1)}, bf16[1024,64]{0,1:T(8,128)(2,1)}, u32[]{:S(2)}) copy-start(bf16[1024,64]{0,1:T(8,128)(2,1)} %fusion.20) | copy-start | bytes 393220
  143.8 28.0 %copy-start.5 = (bf16[1024,64]{0,1:T(8,128)(2,1)S(1)}, bf16[1024,64]{0,1:T(8,128)(2,1)}, u32[]{:S(2)}) copy-start(bf16[1024,64]{0,1:T(8,128)(2,1)} %copy-done.4) | copy-start | bytes 393220
  143.8 28.0 %copy-start.8 = (bf16[1,64,1024]{2,1,0:T(8,128)(2,1)S(1)}, bf16[1,64,1024]{2,1,0:T(8,128)(2,1)}, u32[]{:S(2)}) copy-start(bf16[1,64,1024]{2,1,0:T(8,128)(2,1)} %param.11) | copy-start | bytes 393220
  143.8 28.0 %collective-permute-start.1 = (bf16[1024,1024]{1,0:T(8,128)(2,1)}, bf16[1024,1024]{1,0:T(8,128)(2,1)S(1)}, u32[]{:S(2)}, u32[]{:S(2)}) collective-permute-start(bf16[1024,1024]{1,0:T(8,128)(2,1)} %fusion.7), channel_id=1, source_target_pairs={{0,16},{16,32},{32,48},{48,64},{64,80},{80,96},{96,112},{112,128},... | collective-permute-start | bytes 6291464 | tf_op jit(solution)/shard_map/ppermute | solution.py:12
  173.0 92.0 %copy-start.6 = (f32[1,64,1024]{2,1,0:T(8,128)S(1)}, f32[1,64,1024]{2,1,0:T(8,128)}, u32[]{:S(2)}) copy-start(f32[1,64,1024]{2,1,0:T(8,128)} %param.7) | copy-start | bytes 786436
  201.9 3.2 %copy-start.1 = (bf16[1024,1024]{0,1:T(8,128)(2,1)S(1)}, bf16[1024,1024]{0,1:T(8,128)(2,1)}, u32[]{:S(2)}) copy-start(bf16[1024,1024]{0,1:T(8,128)(2,1)} %all-gather.9.cloned.1.call-done) | copy-start | bytes 6291460
Sparse Core Ops, SparseCore 0:
  11.0 64.6 all-gather.10
  78.8 59.6 all-gather.12
  142.1 59.6 all-gather.8
  205.3 59.6 all-gather.6
where the time goes:
time: 275 us
  waiting for transfers between devices  231 us (84%)
  matrix products  19.5 us (7%)
  between operations  13.9 us (5%)
  starting transfers between devices  9.41 us (3%)
    all_gather x1, waiting for transfers between devices, body(): piece = lax.all_gather(factor[0], 'panel', axis=0, tiled=True)  67.1 us
    all_gather x1, waiting for transfers between devices, body(): lax.all_gather(partner, 'panel', axis=1, tiled=True)  59.2 us
    all_gather x1, waiting for transfers between devices, body(): odd_full = lax.all_gather(source_odd[0], 'panel', axis=0, tiled=True)  51.5 us
    all_gather x1, waiting for transfers between devices, body(): lax.all_gather(whitened_in, 'panel', axis=1, tiled=True)  28.9 us
    ppermute x2, waiting for transfers between devices, shifted(): return lax.ppermute(value, axis, pairs)  23.1 us
    dot_general x5, matrix products, cross_product(): lax.dot_general(left, right, (((0,), (0,)), ((), ())), preferred_element_...  10.3 us
    ppermute x2, starting transfers between devices, shifted(): return lax.ppermute(value, axis, pairs)  9.26 us
  transfers between devices with their start and end apart: 6, of which 6 were waited for; matrix products, arithmetic and copies ran while one was open for 6% of the time, Pallas kernels for 0%

commit v1 on v0

v1 whole, which is shorter than its diff:
```python
import jax
import jax.numpy as jnp
from jax import lax
from jax.experimental import pallas as pl
from jax.experimental.pallas import tpu as pltpu
from jax.sharding import PartitionSpec as P

MESH = pl.DeviceIdType.MESH
ROWS = 64
N = 1024
KEYS = (
    "a_R", "a_L", "b_Y",
    "fa_R", "fa_L", "ya_0", "ya_L", "ya_R", "b_R", "b_L", "pb_R", "pb_L",
    "fb_R", "fpb_R", "fb_L", "fpb_L", "ya_2",
    "sib_0", "sib_1",
)
NKEYS = len(KEYS)
SWAP0 = 4 * NKEYS
RET0 = SWAP0 + 4
NSEM = RET0 + 16


def nt(left, right):
    return lax.dot_general(left, right, (((1,), (1,)), ((), ())), preferred_element_type=jnp.float32)


def nn(left, right):
    return jnp.dot(left, right, preferred_element_type=jnp.float32)


def kernel(
    kept_ref, cin_ref, cout_ref, w_ref, sk_ref, s_ref, obs_ref,
    block_ref, coup_ref, src_ref,
    fw, fs, fi, fo, cinv, cint, keptv, skv, obsv, cc, xt, vacc, vb, r13, r45,
    send1, send3, send4, send2, send5, recv1, recv3, recv4, recv2, recv5,
    ssem, rsem, lsem,
):
    kept_n = lax.axis_size("tm")
    k = lax.axis_index("tm")
    panel = lax.axis_index("panel")
    x, y = lax.rem(panel, 4), panel // 4
    core = lax.rem(k, 2)
    half = y // 2
    home = core == half
    guest = core != half
    py = jnp.where(home, y, 3 - y)
    pyq = py + 1 - 2 * lax.rem(py, 2)
    job = k - core + half
    mine = py * 4 + x

    right = {"panel": y * 4 + lax.rem(x + 1, 4)}
    left = {"panel": y * 4 + lax.rem(x + 3, 4)}
    across = {"panel": (y + 1 - 2 * lax.rem(y, 2)) * 4 + x}
    sibling = {"tm": k + 1 - 2 * core}
    partner = {"tm": k + 1 - 2 * core, "panel": (3 - y) * 4 + x}
    follower = {"tm": lax.rem(job + 1, kept_n), "panel": mine}
    has_follower = job + 1 < kept_n
    has_leader = k > 0
    before = jnp.maximum(k - 1, 0)
    before_core = lax.rem(before, 2)
    before_home = before_core == half
    leader = {
        "tm": jnp.where(before_home, before, before + 1 - 2 * before_core),
        "panel": jnp.where(before_home, panel, (3 - y) * 4 + x),
    }

    load_cin = pltpu.make_async_copy(cin_ref.at[0], cinv, lsem.at[0])
    load_kept = pltpu.make_async_copy(kept_ref.at[0], keptv, lsem.at[1])
    load_sk = pltpu.make_async_copy(sk_ref.at[0], skv, lsem.at[2])
    load_obs = pltpu.make_async_copy(obs_ref, obsv, lsem.at[3])
    load_cin.start()

    barrier = pltpu.get_barrier_semaphore()
    for peer in (right, left, across, sibling):
        pl.semaphore_signal(barrier, inc=1, device_id=peer, device_id_type=MESH)

    @pl.when(guest)
    def _():
        pl.semaphore_signal(barrier, inc=1, device_id=partner, device_id_type=MESH)

    @pl.when(has_leader)
    def _():
        pl.semaphore_signal(barrier, inc=1, device_id=leader, device_id_type=MESH)

    full = (fw, fs, fi, fo)
    own = (w_ref.at[0], s_ref.at[0], cint, cout_ref.at[0])

    def rows(m, p, r0, n):
        return full[m].at[pl.ds(pl.multiple_of(p * ROWS + r0, 16), n)]

    def home_copy(m):
        return pltpu.make_async_copy(own[m], rows(m, panel, 0, ROWS), lsem.at[4 + m])

    def guest_copy(m):
        return pltpu.make_async_remote_copy(
            src_ref=own[m], dst_ref=rows(m, panel, 0, ROWS),
            send_sem=ssem.at[SWAP0 + m], recv_sem=rsem.at[SWAP0 + m],
            device_id=partner, device_id_type=MESH,
        )

    @pl.when(home)
    def _():
        for m in (0, 1, 3):
            home_copy(m).start()

    load_cin.wait()
    cint[...] = cinv[...].T
    load_kept.start()
    load_sk.start()
    load_obs.start()

    @pl.when(k == 0)
    def _():
        recv2[...] = jnp.zeros_like(recv2)
        recv5[...] = jnp.zeros_like(recv5)

    @pl.when(home)
    def _():
        home_copy(2).start()

    pl.semaphore_wait(barrier, 4 + guest.astype(jnp.int32) + has_follower.astype(jnp.int32))

    @pl.when(guest)
    def _():
        for m in range(4):
            guest_copy(m).start()

    def swapped(m):
        @pl.when(home)
        def _():
            home_copy(m).wait()

        @pl.when(guest)
        def _():
            guest_copy(m).wait_recv()

    copies = {}

    def send(m, key, p, r0, n, peer):
        at = m * NKEYS + KEYS.index(key)
        copy = pltpu.make_async_remote_copy(
            src_ref=rows(m, p, r0, n), dst_ref=rows(m, p, r0, n),
            send_sem=ssem.at[at], recv_sem=rsem.at[at],
            device_id=peer, device_id_type=MESH,
        )
        copy.start()
        copies[m, key] = copy

    def got(m, *keys):
        for key in keys:
            copies[m, key].wait_recv()

    xl, xr, xo = lax.rem(x + 3, 4), lax.rem(x + 1, 4), lax.rem(x + 2, 4)
    row, rowq = py * 4, pyq * 4

    def s1(m):
        swapped(m)
        send(m, "a_R", mine, 0, 32, right)
        send(m, "a_L", mine, 0, 32, left)
        send(m, "b_Y", mine, 32, 32, across)

    def s2(m):
        got(m, "a_R")
        send(m, "fa_R", row + xl, 0, 16, right)
        got(m, "a_L")
        send(m, "fa_L", row + xr, 16, 16, left)
        send(m, "ya_0", mine, 0, 32, across)
        send(m, "b_R", mine, 32, 32, right)
        send(m, "b_L", mine, 32, 32, left)
        send(m, "ya_L", row + xl, 0, 32, across)
        send(m, "ya_R", row + xr, 0, 32, across)
        got(m, "b_Y")
        send(m, "pb_R", rowq + x, 32, 32, right)
        send(m, "pb_L", rowq + x, 32, 32, left)

    def s3(m):
        got(m, "fa_R", "fa_L")
        send(m, "ya_2", row + xo, 0, 32, across)
        got(m, "b_R")
        send(m, "fb_R", row + xl, 32, 16, right)
        got(m, "b_L")
        send(m, "fb_L", row + xr, 48, 16, left)
        got(m, "pb_R")
        send(m, "fpb_R", rowq + xl, 32, 16, right)
        got(m, "pb_L")
        send(m, "fpb_L", rowq + xr, 48, 16, left)

    def s4(m):
        got(m, "fb_R", "fb_L")
        send(m, "sib_0", row, 0, 4 * ROWS, sibling)
        got(m, "ya_0", "ya_L", "ya_R", "fpb_R", "fpb_L", "ya_2")
        send(m, "sib_1", rowq, 0, 4 * ROWS, sibling)

    def s5(m):
        got(m, "sib_0", "sib_1")

    def back(at, src, dst, peer):
        return pltpu.make_async_remote_copy(
            src_ref=src, dst_ref=dst, send_sem=ssem.at[RET0 + at], recv_sem=rsem.at[RET0 + at],
            device_id=peer, device_id_type=MESH,
        )

    ret4 = back(0, send4, recv4, partner)
    ret5 = back(1, send5, recv5, follower)
    cols = [pl.ds(256 * i, 256) for i in range(4)]
    ret1 = [back(2 + i, send1.at[:, cols[i]], recv1.at[:, cols[i]], partner) for i in range(4)]
    ret3 = [back(6 + i, send3.at[:, cols[i]], recv3.at[:, cols[i]], partner) for i in range(4)]
    ret2 = [back(10 + i, send2.at[:, cols[i]], recv2.at[:, cols[i]], follower) for i in range(4)]

    s1(0)
    s1(1)
    s1(2)
    s2(0)
    s1(3)
    s2(1)
    s3(0)
    s2(2)
    s3(1)
    s4(0)
    s2(3)
    cc[0:ROWS, :] = fi[pl.ds(pl.multiple_of(mine * ROWS, ROWS), ROWS), :]
    cc[ROWS:, :] = fo[pl.ds(pl.multiple_of(mine * ROWS, ROWS), ROWS), :]
    s5(0)
    for i in range(4):
        part = fw[cols[i], :]
        xt[...] = nt(cc[...], part).astype(jnp.bfloat16)
        if i == 0:
            vacc[...] = nn(xt[...], part)
        else:
            vacc[...] += nn(xt[...], part)
    vb[...] = vacc[...].astype(jnp.bfloat16)
    s3(2)
    s4(1)
    s3(3)
    s5(1)
    for i in range(4):
        part = nn(vb[:, cols[i]], fs[cols[i], :])
        if i == 0:
            r45[...] = part
        else:
            r45[...] += part
    send5[...] = r45[ROWS:, :].astype(jnp.bfloat16)

    @pl.when(has_follower)
    def _():
        ret5.start()

    @pl.when(guest)
    def _():
        send4[...] = r45[:ROWS, :].astype(jnp.bfloat16)
        ret4.start()

    s4(2)
    s5(2)
    for i in range(4):
        r13[:, cols[i]] = nt(vb[...], fi[cols[i], :])

        @pl.when(guest)
        def _():
            send1[:, cols[i]] = r13[:ROWS, cols[i]].astype(jnp.bfloat16)
            send3[:, cols[i]] = r13[ROWS:, cols[i]].astype(jnp.bfloat16)
            ret1[i].start()
            ret3[i].start()

    s4(3)
    s5(3)
    for i in range(4):
        send2[:, cols[i]] = nt(vb[ROWS:, :], fo[cols[i], :]).astype(jnp.bfloat16)

        @pl.when(has_follower)
        def _():
            ret2[i].start()

    load_kept.wait()
    load_sk.wait()
    load_obs.wait()

    @pl.when(has_leader)
    def _():
        ret5.wait_recv()

    @pl.when(home)
    def _():
        src_ref[0] = skv[...].astype(jnp.float32) - recv5[...].astype(jnp.float32) - r45[:ROWS, :]
        coup_ref[0] = -r13[ROWS:, :]
        keptv[...] = keptv[...] - r13[:ROWS, :]

    @pl.when(guest)
    def _():
        ret4.wait_recv()
        src_ref[0] = (
            skv[...].astype(jnp.float32) - recv5[...].astype(jnp.float32) - recv4[...].astype(jnp.float32)
        )
        for i in range(4):
            ret3[i].wait_recv()
        coup_ref[0] = -recv3[...].astype(jnp.float32)
        for i in range(4):
            ret1[i].wait_recv()
        keptv[...] = keptv[...] - recv1[...].astype(jnp.float32)

    at = pl.ds(pl.multiple_of(panel // 2 * 128, 128), 128)
    twice = 2.0 * obsv[...].astype(jnp.float32)
    twice = jnp.concatenate([twice, twice], axis=1)
    on = lax.broadcasted_iota(jnp.int32, (ROWS, 128), 1) == (
        lax.broadcasted_iota(jnp.int32, (ROWS, 128), 0) + ROWS * lax.rem(panel, 2)
    )
    keptv[:, at] = keptv[:, at] + jnp.where(on, jnp.broadcast_to(twice, (ROWS, 128)), 0.0)

    @pl.when(has_leader)
    def _():
        for i in range(4):
            ret2[i].wait_recv()

    block_ref[0] = keptv[...] - recv2[...].astype(jnp.float32)

    for copy in copies.values():
        copy.wait_send()

    @pl.when(guest)
    def _():
        for m in range(4):
            guest_copy(m).wait_send()
        ret4.wait_send()
        for i in range(4):
            ret1[i].wait_send()
            ret3[i].wait_send()

    @pl.when(has_follower)
    def _():
        ret5.wait_send()
        for i in range(4):
            ret2[i].wait_send()


def body(*args):
    bf16, f32 = jnp.bfloat16, jnp.float32
    vmem = pltpu.VMEM
    wide = lambda rows, dtype: vmem((rows, N), dtype)
    return pl.pallas_call(
        kernel,
        out_shape=tuple(jax.ShapeDtypeStruct((1, ROWS, N), f32) for _ in range(3)),
        in_specs=[pl.BlockSpec(memory_space=pl.ANY)] * 7,
        out_specs=(pl.BlockSpec(memory_space=pltpu.VMEM),) * 3,
        scratch_shapes=[wide(N, bf16)] * 4
        + [vmem((N, ROWS), bf16), wide(ROWS, bf16), wide(ROWS, f32), wide(ROWS, bf16), vmem((1, ROWS), jnp.int32)]
        + [wide(2 * ROWS, bf16), vmem((2 * ROWS, 256), bf16), wide(2 * ROWS, f32), wide(2 * ROWS, bf16)]
        + [wide(2 * ROWS, f32)] * 2
        + [wide(ROWS, bf16)] * 10
        + [pltpu.SemaphoreType.DMA((NSEM,))] * 2
        + [pltpu.SemaphoreType.DMA((8,))],
        compiler_params=pltpu.CompilerParams(
            collective_id=0, has_side_effects=True, vmem_limit_bytes=40 << 20
        ),
    )(*args)


def solution(mesh):
    return jax.shard_map(
        body,
        mesh=mesh,
        in_specs=(
            P("tm", "panel", None),
            P("tm", None, "panel"),
            P("tm", "panel", None),
            P("tm", "panel", None),
            P("tm", "panel", None),
            P("tm", "panel", None),
            P("tm", "panel"),
        ),
        out_specs=(P("tm", "panel", None), P("tm", "panel", None), P("tm", "panel", None)),
        check_vma=False,
    )
```

time: 275 us -> 56.1 us (0.20)
  waiting for transfers between devices: 231 us -> 0 us
  Pallas kernels: 0 us -> 48.2 us
  matrix products: 19.5 us -> 0 us
  between operations: 13.9 us -> 0.69 us
  starting transfers between devices: 9.41 us -> 0 us
  local copies, waits for them, and re-layouts: 0.7 us -> 6.6 us
    all_gather x4 -> x0, waiting for transfers between devices: 207 us -> none  [the longest x1 67.1 us: body(): piece = lax.all_gather(factor[0], 'panel', axis=0, tiled=True)]
    pallas_call x0 -> x1, Pallas kernels: none -> 48.2 us  [body(): pl.pallas_call(kernel, out_shape=tuple((jax.ShapeDtypeStruct((1, ROWS, N)...]
    ppermute x2 -> x0, waiting for transfers between devices: 23.1 us -> none  [shifted(): return lax.ppermute(value, axis, pairs)]
    dot_general x8 -> x0, matrix products: 19.5 us -> none  [the longest x5 10.3 us: cross_product(): lax.dot_general(left, right, (((0,), (0,)), ((), ())), preferred_element_...]
    ppermute x2 -> x0, starting transfers between devices: 9.26 us -> none  [shifted(): return lax.ppermute(value, axis, pairs)]
    unnamed x20 -> x16, local copies, waits for them, and re-layouts: 0.7 us -> 6.6 us
  transfers between devices with their start and end apart: 6 -> 0, of which waited for: 6 -> 0; matrix products, arithmetic and copies ran while one was open for 6% -> 0% of each run, Pallas kernels for 0% -> 0%
where the time goes in v1:
time: 56.1 us; the launch traced here: 55.4 us
  Pallas kernels  48.2 us (86%)
  local copies, waits for them, and re-layouts  6.6 us (12%)
  between operations  0.69 us (1%)
    pallas_call x1, Pallas kernels, body(): pl.pallas_call(kernel, out_shape=tuple((jax.ShapeDtypeStruct((1, ROWS, N)...  48.2 us
    unnamed x16, local copies, waits for them, and re-layouts  6.6 us

profile of v1, /device:TPU:1, one launch (start us, length us, event | category | flops | bytes accessed | tf_op | source)
XLA Modules:
  0.0 55.4 jit_solution(995672594023440160)
XLA Ops:
  0.6 0.0 copy-start.1
  0.6 0.0 copy-start
  0.7 1.1 %copy.10.cin_ref = bf16[1,1024,64]{2,1,0:T(8,128)(2,1)S(1)} copy(bf16[1,1024,64]{1,2,0:T(8,128)(2,1)} %param.8) | data formatting | bytes 262144 | tf_op args[1]
  1.8 0.0 copy-done.1
  1.8 0.0 copy-done
  1.8 0.0 copy-start.2
  1.8 0.9 %copy-done.2 = bf16[1,64,1024]{2,1,0:T(8,128)(2,1)S(1)} copy-done((bf16[1,64,1024]{2,1,0:T(8,128)(2,1)S(1)}, bf16[1,64,1024]{2,1,0:T(8,128)(2,1)}, u32[]{:S(2)}) %copy-start.2) | copy-done | bytes 131096
  2.7 0.0 copy-start.3
  2.7 0.9 %copy-done.3 = bf16[1,64,1024]{2,1,0:T(8,128)(2,1)S(1)} copy-done((bf16[1,64,1024]{2,1,0:T(8,128)(2,1)S(1)}, bf16[1,64,1024]{2,1,0:T(8,128)(2,1)}, u32[]{:S(2)}) %copy-start.3) | copy-done | bytes 131096
  3.6 0.0 copy-start.4
  3.6 0.9 %copy-done.4 = bf16[1,64,1024]{2,1,0:T(8,128)(2,1)S(1)} copy-done((bf16[1,64,1024]{2,1,0:T(8,128)(2,1)S(1)}, bf16[1,64,1024]{2,1,0:T(8,128)(2,1)}, u32[]{:S(2)}) %copy-start.4) | copy-done | bytes 131096
  4.5 0.0 copy-start.5
  4.5 0.7 %copy-done.5 = s32[1,64]{1,0:T(1,128)S(1)} copy-done((s32[1,64]{1,0:T(1,128)S(1)}, s32[1,64]{1,0:T(1,128)}, u32[]{:S(2)}) %copy-start.5) | copy-done | bytes 280
  5.2 48.2 %shard_map.94 = (f32[1,64,1024]{2,1,0:T(8,128)S(1)}, f32[1,64,1024]{2,1,0:T(8,128)S(1)}, f32[1,64,1024]{2,1,0:T(8,128)S(1)}) custom-call(f32[1,64,1024]{2,1,0:T(8,128)S(1)} %copy-done, bf16[1,1024,64]{2,1,0:T(8,128)(2,1)S(1)} %copy.10.cin_ref, bf16[1,64,1024]{2,1,0:T(8,128)(2,1)S(1)} %copy-done.1, bf16[1,64,1024]{2,1,0:T(8,128)(2,1)S(1)} %copy-done.2, ...), custom_call_target="tpu_custom_call" | custom-call | tf_op jit(solution)/shard_map/pallas_call | solution.py:339
  53.3 0.7 %copy.14 = f32[1,64,1024]{2,1,0:T(8,128)} copy(f32[1,64,1024]{2,1,0:T(8,128)S(1)} %get-tuple-element.6) | data formatting | bytes 524288
  54.0 0.7 %copy.15 = f32[1,64,1024]{2,1,0:T(8,128)} copy(f32[1,64,1024]{2,1,0:T(8,128)S(1)} %get-tuple-element.7) | data formatting | bytes 524288
  54.7 0.7 %copy.16 = f32[1,64,1024]{2,1,0:T(8,128)} copy(f32[1,64,1024]{2,1,0:T(8,128)S(1)} %get-tuple-element.8) | data formatting | bytes 524288
Async XLA Ops:
  0.6 1.1 %copy-start.1 = (bf16[1,64,1024]{2,1,0:T(8,128)(2,1)S(1)}, bf16[1,64,1024]{2,1,0:T(8,128)(2,1)}, u32[]{:S(2)}) copy-start(bf16[1,64,1024]{2,1,0:T(8,128)(2,1)} %cout_ref.1) | copy-start | bytes 393220
  0.6 1.1 %copy-start = (f32[1,64,1024]{2,1,0:T(8,128)S(1)}, f32[1,64,1024]{2,1,0:T(8,128)}, u32[]{:S(2)}) copy-start(f32[1,64,1024]{2,1,0:T(8,128)} %kept_ref.1) | copy-start | bytes 786436
  1.8 0.9 %copy-start.2 = (bf16[1,64,1024]{2,1,0:T(8,128)(2,1)S(1)}, bf16[1,64,1024]{2,1,0:T(8,128)(2,1)}, u32[]{:S(2)}) copy-start(bf16[1,64,1024]{2,1,0:T(8,128)(2,1)} %w_ref.1) | copy-start | bytes 393220
  2.7 0.9 %copy-start.3 = (bf16[1,64,1024]{2,1,0:T(8,128)(2,1)S(1)}, bf16[1,64,1024]{2,1,0:T(8,128)(2,1)}, u32[]{:S(2)}) copy-start(bf16[1,64,1024]{2,1,0:T(8,128)(2,1)} %sk_ref.1) | copy-start | bytes 393220
  3.6 0.9 %copy-start.4 = (bf16[1,64,1024]{2,1,0:T(8,128)(2,1)S(1)}, bf16[1,64,1024]{2,1,0:T(8,128)(2,1)}, u32[]{:S(2)}) copy-start(bf16[1,64,1024]{2,1,0:T(8,128)(2,1)} %s_ref.1) | copy-start | bytes 393220
  4.5 0.7 %copy-start.5 = (s32[1,64]{1,0:T(1,128)S(1)}, s32[1,64]{1,0:T(1,128)}, u32[]{:S(2)}) copy-start(s32[1,64]{1,0:T(1,128)} %obs_ref.1) | copy-start | bytes 772

commit v2 on v1

--- a/solution.py
+++ b/solution.py
@@ -31,7 +31,7 @@
 def kernel(
     kept_ref, cin_ref, cout_ref, w_ref, sk_ref, s_ref, obs_ref,
     block_ref, coup_ref, src_ref,
-    fw, fs, fi, fo, cinv, cint, keptv, skv, obsv, cc, xt, vacc, vb, r13, r45,
+    fw, fs, fi, fo, keptv, skv, obsv, cc, xt, vacc, vb, r13, r45,
     send1, send3, send4, send2, send5, recv1, recv3, recv4, recv2, recv5,
     ssem, rsem, lsem,
 ):
@@ -64,11 +64,9 @@
         "panel": jnp.where(before_home, panel, (3 - y) * 4 + x),
     }
 
-    load_cin = pltpu.make_async_copy(cin_ref.at[0], cinv, lsem.at[0])
     load_kept = pltpu.make_async_copy(kept_ref.at[0], keptv, lsem.at[1])
     load_sk = pltpu.make_async_copy(sk_ref.at[0], skv, lsem.at[2])
     load_obs = pltpu.make_async_copy(obs_ref, obsv, lsem.at[3])
-    load_cin.start()
 
     barrier = pltpu.get_barrier_semaphore()
     for peer in (right, left, across, sibling):
@@ -83,7 +81,7 @@
         pl.semaphore_signal(barrier, inc=1, device_id=leader, device_id_type=MESH)
 
     full = (fw, fs, fi, fo)
-    own = (w_ref.at[0], s_ref.at[0], cint, cout_ref.at[0])
+    own = (w_ref.at[0], s_ref.at[0], cin_ref.at[0], cout_ref.at[0])
 
     def rows(m, p, r0, n):
         return full[m].at[pl.ds(pl.multiple_of(p * ROWS + r0, 16), n)]
@@ -100,11 +98,9 @@
 
     @pl.when(home)
     def _():
-        for m in (0, 1, 3):
+        for m in range(4):
             home_copy(m).start()
 
-    load_cin.wait()
-    cint[...] = cinv[...].T
     load_kept.start()
     load_sk.start()
     load_obs.start()
@@ -113,10 +109,6 @@
     def _():
         recv2[...] = jnp.zeros_like(recv2)
         recv5[...] = jnp.zeros_like(recv5)
-
-    @pl.when(home)
-    def _():
-        home_copy(2).start()
 
     pl.semaphore_wait(barrier, 4 + guest.astype(jnp.int32) + has_follower.astype(jnp.int32))
 
@@ -332,26 +324,44 @@
             ret2[i].wait_send()
 
 
-def body(*args):
+def store(*refs):
+    ins, outs, sem = refs[:3], refs[3:6], refs[6]
+    copies = [pltpu.make_async_copy(ins[i], outs[i], sem.at[i]) for i in range(3)]
+    for copy in copies:
+        copy.start()
+    for copy in copies:
+        copy.wait()
+
+
+def body(kept_block, coupling_in, *rest):
+    args = (kept_block, jnp.swapaxes(coupling_in, 1, 2), *rest)
     bf16, f32 = jnp.bfloat16, jnp.float32
     vmem = pltpu.VMEM
     wide = lambda rows, dtype: vmem((rows, N), dtype)
-    return pl.pallas_call(
+    shapes = tuple(jax.ShapeDtypeStruct((1, ROWS, N), f32) for _ in range(3))
+    results = pl.pallas_call(
         kernel,
-        out_shape=tuple(jax.ShapeDtypeStruct((1, ROWS, N), f32) for _ in range(3)),
-        in_specs=[pl.BlockSpec(memory_space=pl.ANY)] * 7,
+        out_shape=shapes,
+        in_specs=[pl.BlockSpec(memory_space=pltpu.HBM)] * 7,
         out_specs=(pl.BlockSpec(memory_space=pltpu.VMEM),) * 3,
         scratch_shapes=[wide(N, bf16)] * 4
-        + [vmem((N, ROWS), bf16), wide(ROWS, bf16), wide(ROWS, f32), wide(ROWS, bf16), vmem((1, ROWS), jnp.int32)]
+        + [wide(ROWS, f32), wide(ROWS, bf16), vmem((1, ROWS), jnp.int32)]
         + [wide(2 * ROWS, bf16), vmem((2 * ROWS, 256), bf16), wide(2 * ROWS, f32), wide(2 * ROWS, bf16)]
         + [wide(2 * ROWS, f32)] * 2
         + [wide(ROWS, bf16)] * 10
         + [pltpu.SemaphoreType.DMA((NSEM,))] * 2
         + [pltpu.SemaphoreType.DMA((8,))],
         compiler_params=pltpu.CompilerParams(
-            collective_id=0, has_side_effects=True, vmem_limit_bytes=40 << 20
+            collective_id=0, has_side_effects=True, vmem_limit_bytes=62 << 20
         ),
     )(*args)
+    return pl.pallas_call(
+        store,
+        out_shape=shapes,
+        in_specs=[pl.BlockSpec(memory_space=pltpu.VMEM)] * 3,
+        out_specs=(pl.BlockSpec(memory_space=pltpu.HBM),) * 3,
+        scratch_shapes=[pltpu.SemaphoreType.DMA((3,))],
+    )(*results)
 
 
 def solution(mesh):

time: 56.1 us -> 52 us (0.927)
  local copies, waits for them, and re-layouts: 6.6 us -> 0 us
  Pallas kernels: 48.2 us -> 51 us
    unnamed x16 -> x0, local copies, waits for them, and re-layouts: 6.6 us -> none
    pallas_call x1 -> x2, Pallas kernels: 48.2 us -> 51 us  [the longest x1 49 us: body(): pl.pallas_call(kernel, out_shape=shapes, in_specs=[pl.BlockSpec(memory_sp...]
where the time goes in v2:
time: 52 us; the launch traced here: 51.6 us
  Pallas kernels  51 us (98%)
  between operations  0.64 us (1%)
    pallas_call x1, Pallas kernels, body(): pl.pallas_call(kernel, out_shape=shapes, in_specs=[pl.BlockSpec(memory_sp...  49 us
    pallas_call x1, Pallas kernels, body(): pl.pallas_call(store, out_shape=shapes, in_specs=[pl.BlockSpec(memory_spa...  2.01 us

profile of v2, /device:TPU:1, one launch (start us, length us, event | category | flops | bytes accessed | tf_op | source)
XLA Modules:
  0.0 51.6 jit_solution(14381892216285793753)
XLA Ops:
  0.6 49.0 %shard_map.94 = (f32[1,64,1024]{2,1,0:T(8,128)}, f32[1,64,1024]{2,1,0:T(8,128)}, f32[1,64,1024]{2,1,0:T(8,128)}) custom-call(f32[1,64,1024]{2,1,0:T(8,128)} %kept_ref.1, bf16[1,64,1024]{2,1,0:T(8,128)(2,1)} %bitcast.1, bf16[1,64,1024]{2,1,0:T(8,128)(2,1)} %cout_ref.1, bf16[1,64,1024]{2,1,0:T(8,128)(2,1)} %w_ref.1, bf16[1,64,1024]{2,1,0:T(8,128)(2,1)} %sk_ref.1, ...), custom_call_target="tpu_custom_call" | custom-call | tf_op jit(solution)/shard_map/pallas_call | solution.py:342
  49.6 2.0 %shard_map.95 = (f32[1,64,1024]{2,1,0:T(8,128)}, f32[1,64,1024]{2,1,0:T(8,128)}, f32[1,64,1024]{2,1,0:T(8,128)}) custom-call(f32[1,64,1024]{2,1,0:T(8,128)} %get-tuple-element.6.refs_0_, f32[1,64,1024]{2,1,0:T(8,128)} %get-tuple-element.7.refs_1_, f32[1,64,1024]{2,1,0:T(8,128)} %get-tuple-element.8.refs_2_), custom_call_target="tpu_custom_call" | custom-call | tf_op jit(solution)/shard_map/pallas_call | solution.py:358

commit v3 on v2

v3 whole, which is shorter than its diff:
```python
import jax
import jax.numpy as jnp
from jax import lax
from jax.experimental import pallas as pl
from jax.experimental.pallas import tpu as pltpu
from jax.sharding import PartitionSpec as P

MESH = pl.DeviceIdType.MESH
ROWS = 64
N = 1024
KEYS = (
    "a_R", "a_L", "b_Y",
    "fa_R", "fa_L", "ya_0", "ya_L", "ya_R", "b_R", "b_L", "pb_R", "pb_L",
    "fb_R", "fpb_R", "fb_L", "fpb_L", "ya_2",
    "sib_0", "sib_x", "sib_l", "sib_r", "sib_o",
)
NKEYS = len(KEYS)
SWAP0 = 4 * NKEYS
RET0 = SWAP0 + 4
NSEM = RET0 + 14
SPLIT = ((32, 16, 16),) * 4


SEQ = (('s1', 0), ('s1', 1), ('s1', 2), ('o2', 0), ('s2', 0), ('s1', 3), ('o2', 1), ('s2', 1), ('s3', 0), ('o2', 2), ('s2', 2), ('s3', 1), ('s4a', 0), ('s4b', 0), ('o2', 3), ('s2', 3), ('c0', 0), ('s3', 2), ('s4a', 1), ('s4b', 1), ('c1', 1), ('s3', 3), ('s4a', 2), ('s4b', 2), ('c2', 2))


def nt(left, right):
    return lax.dot_general(left, right, (((1,), (1,)), ((), ())), preferred_element_type=jnp.float32)


def nn(left, right):
    return jnp.dot(left, right, preferred_element_type=jnp.float32)


def kernel(
    kept_ref, cin_ref, cout_ref, w_ref, sk_ref, s_ref, obs_ref,
    block_ref, coup_ref, src_ref,
    fw, fs, fo, fi, keptv, skv, obsv, cc, xt, vacc, vb, r45,
    send1, send3, send4, send2, send5, recv1, recv3, recv4, recv2, recv5,
    ssem, rsem, lsem, ready,
):
    kept_n = lax.axis_size("tm")
    k = lax.axis_index("tm")
    panel = lax.axis_index("panel")
    x, y = lax.rem(panel, 4), panel // 4
    core = lax.rem(k, 2)
    half = y // 2
    home = core == half
    guest = core != half
    py = jnp.where(home, y, 3 - y)
    pyq = py + 1 - 2 * lax.rem(py, 2)
    job = k - core + half
    mine = py * 4 + x

    right = {"panel": y * 4 + lax.rem(x + 1, 4)}
    left = {"panel": y * 4 + lax.rem(x + 3, 4)}
    across = {"panel": (y + 1 - 2 * lax.rem(y, 2)) * 4 + x}
    sibling = {"tm": k + 1 - 2 * core}
    partner = {"tm": k + 1 - 2 * core, "panel": (3 - y) * 4 + x}
    follower = {"tm": lax.rem(job + 1, kept_n), "panel": mine}
    has_follower = job + 1 < kept_n
    has_leader = k > 0
    before = jnp.maximum(k - 1, 0)
    before_core = lax.rem(before, 2)
    before_home = before_core == half
    leader = {
        "tm": jnp.where(before_home, before, before + 1 - 2 * before_core),
        "panel": jnp.where(before_home, panel, (3 - y) * 4 + x),
    }

    load_kept = pltpu.make_async_copy(kept_ref.at[0], keptv, lsem.at[0])
    load_sk = pltpu.make_async_copy(sk_ref.at[0], skv, lsem.at[1])
    load_obs = pltpu.make_async_copy(obs_ref, obsv, lsem.at[2])

    barrier = pltpu.get_barrier_semaphore()
    for peer in (right, left, across, sibling):
        pl.semaphore_signal(barrier, inc=1, device_id=peer, device_id_type=MESH)

    @pl.when(guest)
    def _():
        pl.semaphore_signal(barrier, inc=1, device_id=partner, device_id_type=MESH)

    @pl.when(has_follower)
    def _():
        pl.semaphore_signal(barrier, inc=1, device_id=follower, device_id_type=MESH)

    full = (fw, fs, fo, fi)
    own = (w_ref.at[0], s_ref.at[0], cout_ref.at[0], cin_ref.at[0])

    def rows(m, p, r0, n):
        return full[m].at[pl.ds(pl.multiple_of(p * ROWS + r0, 16), n)]

    def home_copy(m):
        return pltpu.make_async_copy(own[m], rows(m, panel, 0, ROWS), lsem.at[3 + m])

    def guest_copy(m):
        return pltpu.make_async_remote_copy(
            src_ref=own[m], dst_ref=rows(m, panel, 0, ROWS),
            send_sem=ssem.at[SWAP0 + m], recv_sem=rsem.at[SWAP0 + m],
            device_id=partner, device_id_type=MESH,
        )

    @pl.when(home)
    def _():
        for m in range(4):
            home_copy(m).start()

    load_kept.start()
    load_sk.start()
    load_obs.start()

    @pl.when(k == 0)
    def _():
        recv2[...] = jnp.zeros_like(recv2)
        recv5[...] = jnp.zeros_like(recv5)

    pl.semaphore_wait(barrier, 4 + guest.astype(jnp.int32) + has_leader.astype(jnp.int32))

    @pl.when(guest)
    def _():
        for m in range(4):
            guest_copy(m).start()

    @pl.when(has_leader)
    def _():
        pl.semaphore_signal(ready, inc=1, device_id=leader, device_id_type=MESH)

    def swapped(m):
        @pl.when(home)
        def _():
            home_copy(m).wait()

        @pl.when(guest)
        def _():
            guest_copy(m).wait_recv()

    copies = {}

    def send(m, key, p, r0, n, peer):
        if n == 0:
            return
        at = m * NKEYS + KEYS.index(key)
        copy = pltpu.make_async_remote_copy(
            src_ref=rows(m, p, r0, n), dst_ref=rows(m, p, r0, n),
            send_sem=ssem.at[at], recv_sem=rsem.at[at],
            device_id=peer, device_id_type=MESH,
        )
        copy.start()
        copies[m, key] = copy

    def got(m, *keys):
        for key in keys:
            if (m, key) in copies:
                copies[m, key].wait_recv()

    xl, xr, xo = lax.rem(x + 3, 4), lax.rem(x + 1, 4), lax.rem(x + 2, 4)
    row, rowq = py * 4, pyq * 4

    def s1(m):
        a = SPLIT[m][0]
        swapped(m)
        send(m, "a_R", mine, 0, a, right)
        send(m, "a_L", mine, 0, a, left)
        send(m, "b_Y", mine, a, ROWS - a, across)

    def o2(m):
        a = SPLIT[m][0]
        send(m, "ya_0", mine, 0, a, across)
        send(m, "b_R", mine, a, ROWS - a, right)
        send(m, "b_L", mine, a, ROWS - a, left)

    def s2(m):
        a, ra, _ = SPLIT[m]
        got(m, "a_R")
        send(m, "fa_R", row + xl, 0, ra, right)
        got(m, "a_L")
        send(m, "fa_L", row + xr, ra, a - ra, left)
        send(m, "ya_L", row + xl, 0, a, across)
        send(m, "ya_R", row + xr, 0, a, across)
        got(m, "b_Y")
        send(m, "pb_R", rowq + x, a, ROWS - a, right)
        send(m, "pb_L", rowq + x, a, ROWS - a, left)

    def s3(m):
        a, _, rb = SPLIT[m]
        got(m, "fa_R", "fa_L")
        send(m, "ya_2", row + xo, 0, a, across)
        got(m, "b_R")
        send(m, "fb_R", row + xl, a, rb, right)
        got(m, "b_L")
        send(m, "fb_L", row + xr, a + rb, ROWS - a - rb, left)
        got(m, "pb_R")
        send(m, "fpb_R", rowq + xl, a, rb, right)
        got(m, "pb_L")
        send(m, "fpb_L", rowq + xr, a + rb, ROWS - a - rb, left)

    def s4a(m):
        got(m, "fb_R", "fb_L")
        send(m, "sib_0", row, 0, 4 * ROWS, sibling)

    def s4b(m):
        got(m, "ya_0")
        send(m, "sib_x", rowq + x, 0, ROWS, sibling)
        got(m, "ya_L")
        send(m, "sib_l", rowq + xl, 0, ROWS, sibling)
        got(m, "ya_R")
        send(m, "sib_r", rowq + xr, 0, ROWS, sibling)
        got(m, "fpb_R", "fpb_L", "ya_2")
        send(m, "sib_o", rowq + xo, 0, ROWS, sibling)

    def s5(m):
        got(m, "sib_0", "sib_x", "sib_l", "sib_r", "sib_o")

    def back(at, src, dst, peer):
        return pltpu.make_async_remote_copy(
            src_ref=src, dst_ref=dst, send_sem=ssem.at[RET0 + at], recv_sem=rsem.at[RET0 + at],
            device_id=peer, device_id_type=MESH,
        )

    def span(p):
        return pl.ds(pl.multiple_of(p * 256, 256), 256)

    cols = [pl.ds(256 * i, 256) for i in range(4)]
    groups = [span(p) for p in (py, 3 - py, pyq, 3 - pyq)]
    theirs = [span(p) for p in (3 - py, py, 3 - pyq, pyq)]
    ret4 = back(0, send4, recv4, partner)
    ret5 = back(1, send5, recv5, follower)
    ret1 = [back(2 + i, send1.at[:, groups[i]], recv1.at[:, groups[i]], partner) for i in range(4)]
    ret3 = [back(6 + i, send3.at[:, groups[i]], recv3.at[:, groups[i]], partner) for i in range(4)]
    ret2 = [back(10 + i, send2.at[:, cols[i]], recv2.at[:, cols[i]], follower) for i in range(4)]

    def c0(m):
        s5(m)
        cc[0:ROWS, :] = fi[pl.ds(pl.multiple_of(mine * ROWS, ROWS), ROWS), :]
        cc[ROWS:, :] = fo[pl.ds(pl.multiple_of(mine * ROWS, ROWS), ROWS), :]
        for i in range(4):
            part = fw[cols[i], :]
            xt[...] = nt(cc[...], part).astype(jnp.bfloat16)
            if i == 0:
                vacc[...] = nn(xt[...], part)
            else:
                vacc[...] += nn(xt[...], part)
        vb[...] = vacc[...].astype(jnp.bfloat16)

    def c1(m):
        s5(m)
        for i in range(4):
            part = nn(vb[:, cols[i]], fs[cols[i], :])
            if i == 0:
                r45[...] = part
            else:
                r45[...] += part
        send5[...] = r45[ROWS:, :].astype(jnp.bfloat16)

        @pl.when(has_follower)
        def _():
            pl.semaphore_wait(ready, 1)
            ret5.start()

        @pl.when(guest)
        def _():
            send4[...] = r45[:ROWS, :].astype(jnp.bfloat16)
            ret4.start()


    def c2(m):
        s5(m)
        for i in range(4):
            send2[:, cols[i]] = nt(vb[ROWS:, :], fo[cols[i], :]).astype(jnp.bfloat16)

            @pl.when(has_follower)
            def _():
                ret2[i].start()


    for step, m in SEQ:
        {"s1": s1, "o2": o2, "s2": s2, "s3": s3, "s4a": s4a, "s4b": s4b, "c0": c0, "c1": c1, "c2": c2}[step](m)
    s4a(3)
    load_kept.wait()
    load_sk.wait()
    load_obs.wait()
    at = pl.ds(pl.multiple_of(panel // 2 * 128, 128), 128)
    twice = 2.0 * obsv[...].astype(jnp.float32)
    twice = jnp.concatenate([twice, twice], axis=1)
    on = lax.broadcasted_iota(jnp.int32, (ROWS, 128), 1) == (
        lax.broadcasted_iota(jnp.int32, (ROWS, 128), 0) + ROWS * lax.rem(panel, 2)
    )
    keptv[:, at] = keptv[:, at] + jnp.where(on, jnp.broadcast_to(twice, (ROWS, 128)), 0.0)

    @pl.when(has_leader)
    def _():
        ret5.wait_recv()

    @pl.when(home)
    def _():
        src_ref[0] = skv[...].astype(jnp.float32) - recv5[...].astype(jnp.float32) - r45[:ROWS, :]

    @pl.when(guest)
    def _():
        ret4.wait_recv()
        src_ref[0] = skv[...].astype(jnp.float32) - recv5[...].astype(jnp.float32) - recv4[...].astype(jnp.float32)

    s4b(3)

    @pl.when(has_leader)
    def _():
        for i in range(4):
            ret2[i].wait_recv()

    keptv[...] = keptv[...] - recv2[...].astype(jnp.float32)
    for i, keys in enumerate(((), ("sib_0",), (), ("sib_x", "sib_l", "sib_r", "sib_o"))):
        got(3, *keys)
        both = nt(vb[...], fi[groups[i], :])

        @pl.when(home)
        def _():
            block_ref[0, :, groups[i]] = keptv[:, groups[i]] - both[:ROWS, :]
            coup_ref[0, :, groups[i]] = -both[ROWS:, :]

        @pl.when(guest)
        def _():
            send1[:, groups[i]] = both[:ROWS, :].astype(jnp.bfloat16)
            send3[:, groups[i]] = both[ROWS:, :].astype(jnp.bfloat16)
            ret1[i].start()
            ret3[i].start()

    @pl.when(guest)
    def _():
        for i in range(4):
            ret1[i].wait_recv()
            block_ref[0, :, theirs[i]] = keptv[:, theirs[i]] - recv1[:, theirs[i]].astype(jnp.float32)
            ret3[i].wait_recv()
            coup_ref[0, :, theirs[i]] = -recv3[:, theirs[i]].astype(jnp.float32)

    for copy in copies.values():
        copy.wait_send()

    @pl.when(guest)
    def _():
        for m in range(4):
            guest_copy(m).wait_send()
        ret4.wait_send()
        for i in range(4):
            ret1[i].wait_send()
            ret3[i].wait_send()

    @pl.when(has_follower)
    def _():
        ret5.wait_send()
        for i in range(4):
            ret2[i].wait_send()


def store(*refs):
    ins, outs, sem = refs[:3], refs[3:6], refs[6]
    puts = [pltpu.make_async_copy(ins[i], outs[i], sem.at[i]) for i in range(3)]
    for copy in puts:
        copy.start()
    for copy in puts:
        copy.wait()


def body(kept_block, coupling_in, *rest):
    args = (kept_block, jnp.swapaxes(coupling_in, 1, 2), *rest)
    args = tuple(pltpu.with_memory_space_constraint(a, pltpu.HBM) for a in args)
    bf16, f32 = jnp.bfloat16, jnp.float32
    vmem = pltpu.VMEM
    wide = lambda rows, dtype: vmem((rows, N), dtype)
    shapes = tuple(jax.ShapeDtypeStruct((1, ROWS, N), f32) for _ in range(3))
    results = pl.pallas_call(
        kernel,
        out_shape=shapes,
        in_specs=[pl.BlockSpec(memory_space=pltpu.HBM)] * 7,
        out_specs=(pl.BlockSpec(memory_space=pltpu.VMEM),) * 3,
        scratch_shapes=[wide(N, bf16)] * 4
        + [wide(ROWS, f32), wide(ROWS, bf16), vmem((1, ROWS), jnp.int32)]
        + [wide(2 * ROWS, bf16), vmem((2 * ROWS, 256), bf16), wide(2 * ROWS, f32), wide(2 * ROWS, bf16)]
        + [wide(2 * ROWS, f32)]
        + [wide(ROWS, bf16)] * 10
        + [pltpu.SemaphoreType.DMA((NSEM,))] * 2
        + [pltpu.SemaphoreType.DMA((16,)), pltpu.SemaphoreType.REGULAR],
        compiler_params=pltpu.CompilerParams(
            collective_id=0, has_side_effects=True, vmem_limit_bytes=40 << 20
        ),
    )(*args)
    return pl.pallas_call(
        store,
        out_shape=shapes,
        in_specs=[pl.BlockSpec(memory_space=pl.ANY)] * 3,
        out_specs=(pl.BlockSpec(memory_space=pltpu.HBM),) * 3,
        scratch_shapes=[pltpu.SemaphoreType.DMA((3,))],
        compiler_params=pltpu.CompilerParams(vmem_limit_bytes=16 << 20),
    )(*results)


def solution(mesh):
    return jax.shard_map(
        body,
        mesh=mesh,
        in_specs=(
            P("tm", "panel", None),
            P("tm", None, "panel"),
            P("tm", "panel", None),
            P("tm", "panel", None),
            P("tm", "panel", None),
            P("tm", "panel", None),
            P("tm", "panel"),
        ),
        out_specs=(P("tm", "panel", None), P("tm", "panel", None), P("tm", "panel", None)),
        check_vma=False,
    )
```

time: 52 us -> 50.6 us (0.973)
  the two profiles are of different devices: /device:TPU:1 before, /device:TPU:385 now
where the time goes in v3:
time: 50.6 us; the launch traced here: 50.5 us
  Pallas kernels  49.8 us (98%)
  between operations  0.64 us (1%)
    pallas_call x1, Pallas kernels, body(): pl.pallas_call(kernel, out_shape=shapes, in_specs=[pl.BlockSpec(memory_sp...  48.9 us

profile of v3, /device:TPU:385, one launch (start us, length us, event | category | flops | bytes accessed | tf_op | source)
XLA Modules:
  0.0 50.5 jit_solution(3176360886031217833)
XLA Ops:
  0.6 48.9 %shard_map.94 = (f32[1,64,1024]{2,1,0:T(8,128)S(1)}, f32[1,64,1024]{2,1,0:T(8,128)S(1)}, f32[1,64,1024]{2,1,0:T(8,128)S(1)}) custom-call(f32[1,64,1024]{2,1,0:T(8,128)} %kept_ref.1, bf16[1,64,1024]{2,1,0:T(8,128)(2,1)} %bitcast.1, bf16[1,64,1024]{2,1,0:T(8,128)(2,1)} %cout_ref.1, bf16[1,64,1024]{2,1,0:T(8,128)(2,1)} %w_ref.1, bf16[1,64,1024]{2,1,0:T(8,128)(2,1)} %sk_ref.1, ...), custom_call_target="tpu_custom_call" | custom-call | tf_op jit(solution)/shard_map/pallas_call | solution.py:370
  49.5 0.9 %shard_map.95 = (f32[1,64,1024]{2,1,0:T(8,128)}, f32[1,64,1024]{2,1,0:T(8,128)}, f32[1,64,1024]{2,1,0:T(8,128)}) custom-call(f32[1,64,1024]{2,1,0:T(8,128)S(1)} %get-tuple-element.6.refs_0_, f32[1,64,1024]{2,1,0:T(8,128)S(1)} %get-tuple-element.7.refs_1_, f32[1,64,1024]{2,1,0:T(8,128)S(1)} %get-tuple-element.8.refs_2_), custom_call_target="tpu_custom_call" | custom-call | tf_op jit(solution)/shard_map/pallas_call | solution.py:386

commit v4 on v3

--- a/solution.py
+++ b/solution.py
@@ -17,7 +17,7 @@
 NKEYS = len(KEYS)
 SWAP0 = 4 * NKEYS
 RET0 = SWAP0 + 4
-NSEM = RET0 + 14
+NSEM = RET0 + 10
 SPLIT = ((32, 16, 16),) * 4
 
 
@@ -36,7 +36,7 @@
     kept_ref, cin_ref, cout_ref, w_ref, sk_ref, s_ref, obs_ref,
     block_ref, coup_ref, src_ref,
     fw, fs, fo, fi, keptv, skv, obsv, cc, xt, vacc, vb, r45,
-    send1, send3, send4, send2, send5, recv1, recv3, recv4, recv2, recv5,
+    send13, send4, send2, send5, recv13, recv4, recv2, recv5,
     ssem, rsem, lsem, ready,
 ):
     kept_n = lax.axis_size("tm")
@@ -225,9 +225,8 @@
     theirs = [span(p) for p in (3 - py, py, 3 - pyq, pyq)]
     ret4 = back(0, send4, recv4, partner)
     ret5 = back(1, send5, recv5, follower)
-    ret1 = [back(2 + i, send1.at[:, groups[i]], recv1.at[:, groups[i]], partner) for i in range(4)]
-    ret3 = [back(6 + i, send3.at[:, groups[i]], recv3.at[:, groups[i]], partner) for i in range(4)]
-    ret2 = [back(10 + i, send2.at[:, cols[i]], recv2.at[:, cols[i]], follower) for i in range(4)]
+    ret13 = [back(2 + i, send13.at[:, groups[i]], recv13.at[:, groups[i]], partner) for i in range(4)]
+    ret2 = [back(6 + i, send2.at[:, cols[i]], recv2.at[:, cols[i]], follower) for i in range(4)]
 
     def c0(m):
         s5(m)
@@ -275,7 +274,32 @@
 
     for step, m in SEQ:
         {"s1": s1, "o2": o2, "s2": s2, "s3": s3, "s4a": s4a, "s4b": s4b, "c0": c0, "c1": c1, "c2": c2}[step](m)
+    def c3(i):
+        both = nt(vb[...], fi[groups[i], :])
+
+        @pl.when(home)
+        def _():
+            block_ref[0, :, groups[i]] = -both[:ROWS, :]
+            coup_ref[0, :, groups[i]] = -both[ROWS:, :]
+
+        @pl.when(guest)
+        def _():
+            send13[:, groups[i]] = both.astype(jnp.bfloat16)
+            ret13[i].start()
+
     s4a(3)
+    c3(0)
+    got(3, "ya_0")
+    send(3, "sib_x", rowq + x, 0, ROWS, sibling)
+    got(3, "ya_L")
+    send(3, "sib_l", rowq + xl, 0, ROWS, sibling)
+    got(3, "ya_R")
+    send(3, "sib_r", rowq + xr, 0, ROWS, sibling)
+    got(3, "sib_0")
+    c3(1)
+    got(3, "fpb_R", "fpb_L", "ya_2")
+    send(3, "sib_o", rowq + xo, 0, ROWS, sibling)
+    c3(2)
     load_kept.wait()
     load_sk.wait()
     load_obs.wait()
@@ -300,7 +324,8 @@
         ret4.wait_recv()
         src_ref[0] = skv[...].astype(jnp.float32) - recv5[...].astype(jnp.float32) - recv4[...].astype(jnp.float32)
 
-    s4b(3)
+    got(3, "sib_x", "sib_l", "sib_r", "sib_o")
+    c3(3)
 
     @pl.when(has_leader)
     def _():
@@ -308,29 +333,17 @@
             ret2[i].wait_recv()
 
     keptv[...] = keptv[...] - recv2[...].astype(jnp.float32)
-    for i, keys in enumerate(((), ("sib_0",), (), ("sib_x", "sib_l", "sib_r", "sib_o"))):
-        got(3, *keys)
-        both = nt(vb[...], fi[groups[i], :])
-
-        @pl.when(home)
-        def _():
-            block_ref[0, :, groups[i]] = keptv[:, groups[i]] - both[:ROWS, :]
-            coup_ref[0, :, groups[i]] = -both[ROWS:, :]
-
-        @pl.when(guest)
-        def _():
-            send1[:, groups[i]] = both[:ROWS, :].astype(jnp.bfloat16)
-            send3[:, groups[i]] = both[ROWS:, :].astype(jnp.bfloat16)
-            ret1[i].start()
-            ret3[i].start()
+
+    @pl.when(home)
+    def _():
+        block_ref[0] = keptv[...] + block_ref[0]
 
     @pl.when(guest)
     def _():
         for i in range(4):
-            ret1[i].wait_recv()
-            block_ref[0, :, theirs[i]] = keptv[:, theirs[i]] - recv1[:, theirs[i]].astype(jnp.float32)
-            ret3[i].wait_recv()
-            coup_ref[0, :, theirs[i]] = -recv3[:, theirs[i]].astype(jnp.float32)
+            ret13[i].wait_recv()
+            block_ref[0, :, theirs[i]] = keptv[:, theirs[i]] - recv13[:ROWS, theirs[i]].astype(jnp.float32)
+            coup_ref[0, :, theirs[i]] = -recv13[ROWS:, theirs[i]].astype(jnp.float32)
 
     for copy in copies.values():
         copy.wait_send()
@@ -341,8 +354,7 @@
             guest_copy(m).wait_send()
         ret4.wait_send()
         for i in range(4):
-            ret1[i].wait_send()
-            ret3[i].wait_send()
+            ret13[i].wait_send()
 
     @pl.when(has_follower)
     def _():
@@ -376,7 +388,7 @@
         + [wide(ROWS, f32), wide(ROWS, bf16), vmem((1, ROWS), jnp.int32)]
         + [wide(2 * ROWS, bf16), vmem((2 * ROWS, 256), bf16), wide(2 * ROWS, f32), wide(2 * ROWS, bf16)]
         + [wide(2 * ROWS, f32)]
-        + [wide(ROWS, bf16)] * 10
+        + [wide(2 * ROWS, bf16)] + [wide(ROWS, bf16)] * 3 + [wide(2 * ROWS, bf16)] + [wide(ROWS, bf16)] * 3
         + [pltpu.SemaphoreType.DMA((NSEM,))] * 2
         + [pltpu.SemaphoreType.DMA((16,)), pltpu.SemaphoreType.REGULAR],
         compiler_params=pltpu.CompilerParams(

time: 50.6 us -> 49 us (0.968)
  the two profiles are of different devices: /device:TPU:385 before, /device:TPU:1 now
where the time goes in v4:
time: 49 us; the launch traced here: 48.5 us
  Pallas kernels  47.8 us (98%)
  between operations  0.64 us (1%)
    pallas_call x1, Pallas kernels, body(): pl.pallas_call(kernel, out_shape=shapes, in_specs=[pl.BlockSpec(memory_sp...  46.9 us

profile of v4, /device:TPU:1, one launch (start us, length us, event | category | flops | bytes accessed | tf_op | source)
XLA Modules:
  0.0 48.5 jit_solution(17554031776902689513)
XLA Ops:
  0.6 46.9 %shard_map.94 = (f32[1,64,1024]{2,1,0:T(8,128)S(1)}, f32[1,64,1024]{2,1,0:T(8,128)S(1)}, f32[1,64,1024]{2,1,0:T(8,128)S(1)}) custom-call(f32[1,64,1024]{2,1,0:T(8,128)} %kept_ref.1, bf16[1,64,1024]{2,1,0:T(8,128)(2,1)} %bitcast.1, bf16[1,64,1024]{2,1,0:T(8,128)(2,1)} %cout_ref.1, bf16[1,64,1024]{2,1,0:T(8,128)(2,1)} %w_ref.1, bf16[1,64,1024]{2,1,0:T(8,128)(2,1)} %sk_ref.1, ...), custom_call_target="tpu_custom_call" | custom-call | tf_op jit(solution)/shard_map/pallas_call | solution.py:382
  47.6 0.9 %shard_map.95 = (f32[1,64,1024]{2,1,0:T(8,128)}, f32[1,64,1024]{2,1,0:T(8,128)}, f32[1,64,1024]{2,1,0:T(8,128)}) custom-call(f32[1,64,1024]{2,1,0:T(8,128)S(1)} %get-tuple-element.6.refs_0_, f32[1,64,1024]{2,1,0:T(8,128)S(1)} %get-tuple-element.7.refs_1_, f32[1,64,1024]{2,1,0:T(8,128)S(1)} %get-tuple-element.8.refs_2_), custom_call_target="tpu_custom_call" | custom-call | tf_op jit(solution)/shard_map/pallas_call | solution.py:398

commit v5 on v4

--- a/solution.py
+++ b/solution.py
@@ -21,7 +21,7 @@
 SPLIT = ((32, 16, 16),) * 4
 
 
-SEQ = (('s1', 0), ('s1', 1), ('s1', 2), ('o2', 0), ('s2', 0), ('s1', 3), ('o2', 1), ('s2', 1), ('s3', 0), ('o2', 2), ('s2', 2), ('s3', 1), ('s4a', 0), ('s4b', 0), ('o2', 3), ('s2', 3), ('c0', 0), ('s3', 2), ('s4a', 1), ('s4b', 1), ('c1', 1), ('s3', 3), ('s4a', 2), ('s4b', 2), ('c2', 2))
+SEQ = (('s1', 0), ('s1', 1), ('s1', 2), ('o2', 0), ('s2', 0), ('s1', 3), ('o2', 1), ('s2', 1), ('s3', 0), ('o2', 2), ('s2', 2), ('s3', 1), ('s4a', 0), ('s4b', 0), ('o2', 3), ('s2', 3), ('c0', 0), ('c0', 1), ('s3', 2), ('s4a', 1), ('s4b', 1), ('c1', 0), ('c1', 1), ('s3', 3), ('s4a', 2), ('s4b', 2), ('c2', 0), ('c2', 1))
 
 
 def nt(left, right):
@@ -136,7 +136,7 @@
 
     copies = {}
 
-    def send(m, key, p, r0, n, peer):
+    def send(m, key, p, r0, n, peer, start=True):
         if n == 0:
             return
         at = m * NKEYS + KEYS.index(key)
@@ -145,7 +145,8 @@
             send_sem=ssem.at[at], recv_sem=rsem.at[at],
             device_id=peer, device_id_type=MESH,
         )
-        copy.start()
+        if start:
+            copy.start()
         copies[m, key] = copy
 
     def got(m, *keys):
@@ -208,9 +209,6 @@
         got(m, "fpb_R", "fpb_L", "ya_2")
         send(m, "sib_o", rowq + xo, 0, ROWS, sibling)
 
-    def s5(m):
-        got(m, "sib_0", "sib_x", "sib_l", "sib_r", "sib_o")
-
     def back(at, src, dst, peer):
         return pltpu.make_async_remote_copy(
             src_ref=src, dst_ref=dst, send_sem=ssem.at[RET0 + at], recv_sem=rsem.at[RET0 + at],
@@ -220,35 +218,45 @@
     def span(p):
         return pl.ds(pl.multiple_of(p * 256, 256), 256)
 
-    cols = [pl.ds(256 * i, 256) for i in range(4)]
-    groups = [span(p) for p in (py, 3 - py, pyq, 3 - pyq)]
-    theirs = [span(p) for p in (3 - py, py, 3 - pyq, pyq)]
+    spans = [span(p) for p in (py, pyq, 3 - py, 3 - pyq)]
+    groups = [span(p) for p in (py, 3 - py, jnp.where(home, pyq, 3 - pyq), jnp.where(home, 3 - pyq, pyq))]
+    theirs = [span(p) for p in (3 - py, py, pyq, 3 - pyq)]
     ret4 = back(0, send4, recv4, partner)
     ret5 = back(1, send5, recv5, follower)
     ret13 = [back(2 + i, send13.at[:, groups[i]], recv13.at[:, groups[i]], partner) for i in range(4)]
-    ret2 = [back(6 + i, send2.at[:, cols[i]], recv2.at[:, cols[i]], follower) for i in range(4)]
-
-    def c0(m):
-        s5(m)
-        cc[0:ROWS, :] = fi[pl.ds(pl.multiple_of(mine * ROWS, ROWS), ROWS), :]
-        cc[ROWS:, :] = fo[pl.ds(pl.multiple_of(mine * ROWS, ROWS), ROWS), :]
-        for i in range(4):
-            part = fw[cols[i], :]
+    ret2 = [back(6 + i, send2.at[:, spans[i]], recv2.at[:, spans[i]], follower) for i in range(4)]
+
+    def need(m, i):
+        if i == 2:
+            got(m, "sib_0")
+        if i == 3:
+            got(m, "sib_x", "sib_l", "sib_r", "sib_o")
+
+    def c0(half_of):
+        if half_of == 0:
+            cc[0:ROWS, :] = fi[pl.ds(pl.multiple_of(mine * ROWS, ROWS), ROWS), :]
+            cc[ROWS:, :] = fo[pl.ds(pl.multiple_of(mine * ROWS, ROWS), ROWS), :]
+        for i in (2 * half_of, 2 * half_of + 1):
+            need(0, i)
+            part = fw[spans[i], :]
             xt[...] = nt(cc[...], part).astype(jnp.bfloat16)
             if i == 0:
                 vacc[...] = nn(xt[...], part)
             else:
                 vacc[...] += nn(xt[...], part)
-        vb[...] = vacc[...].astype(jnp.bfloat16)
-
-    def c1(m):
-        s5(m)
-        for i in range(4):
-            part = nn(vb[:, cols[i]], fs[cols[i], :])
+        if half_of == 1:
+            vb[...] = vacc[...].astype(jnp.bfloat16)
+
+    def c1(half_of):
+        for i in (2 * half_of, 2 * half_of + 1):
+            need(1, i)
+            part = nn(vb[:, spans[i]], fs[spans[i], :])
             if i == 0:
                 r45[...] = part
             else:
                 r45[...] += part
+        if half_of == 0:
+            return
         send5[...] = r45[ROWS:, :].astype(jnp.bfloat16)
 
         @pl.when(has_follower)
@@ -261,31 +269,36 @@
             send4[...] = r45[:ROWS, :].astype(jnp.bfloat16)
             ret4.start()
 
-
-    def c2(m):
-        s5(m)
-        for i in range(4):
-            send2[:, cols[i]] = nt(vb[ROWS:, :], fo[cols[i], :]).astype(jnp.bfloat16)
+    def c2(half_of):
+        for i in (2 * half_of, 2 * half_of + 1):
+            need(2, i)
+            send2[:, spans[i]] = nt(vb[ROWS:, :], fo[spans[i], :]).astype(jnp.bfloat16)
 
             @pl.when(has_follower)
             def _():
                 ret2[i].start()
 
-
+    steps = {"s1": s1, "o2": o2, "s2": s2, "s3": s3, "s4a": s4a, "s4b": s4b, "c0": c0, "c1": c1, "c2": c2}
     for step, m in SEQ:
-        {"s1": s1, "o2": o2, "s2": s2, "s3": s3, "s4a": s4a, "s4b": s4b, "c0": c0, "c1": c1, "c2": c2}[step](m)
+        steps[step](m)
+
+    def stay(i):
+        both = nt(vb[...], fi[groups[i], :])
+        block_ref[0, :, groups[i]] = -both[:ROWS, :]
+        coup_ref[0, :, groups[i]] = -both[ROWS:, :]
+
+    def give(i):
+        send13[:, groups[i]] = nt(vb[...], fi[groups[i], :]).astype(jnp.bfloat16)
+        ret13[i].start()
+
     def c3(i):
-        both = nt(vb[...], fi[groups[i], :])
-
         @pl.when(home)
         def _():
-            block_ref[0, :, groups[i]] = -both[:ROWS, :]
-            coup_ref[0, :, groups[i]] = -both[ROWS:, :]
+            stay(i)
 
         @pl.when(guest)
         def _():
-            send13[:, groups[i]] = both.astype(jnp.bfloat16)
-            ret13[i].start()
+            give(i)
 
     s4a(3)
     c3(0)
@@ -297,9 +310,24 @@
     send(3, "sib_r", rowq + xr, 0, ROWS, sibling)
     got(3, "sib_0")
     c3(1)
-    got(3, "fpb_R", "fpb_L", "ya_2")
-    send(3, "sib_o", rowq + xo, 0, ROWS, sibling)
-    c3(2)
+    send(3, "sib_o", rowq + xo, 0, ROWS, sibling, False)
+    last = ("fpb_R", "fpb_L", "ya_2")
+    others = ("sib_x", "sib_l", "sib_r", "sib_o")
+
+    @pl.when(home)
+    def _():
+        got(3, *last)
+        copies[3, "sib_o"].start()
+        stay(2)
+
+    @pl.when(guest)
+    def _():
+        got(3, *others)
+        give(2)
+        got(3, *last)
+        copies[3, "sib_o"].start()
+        give(3)
+
     load_kept.wait()
     load_sk.wait()
     load_obs.wait()
@@ -324,8 +352,13 @@
         ret4.wait_recv()
         src_ref[0] = skv[...].astype(jnp.float32) - recv5[...].astype(jnp.float32) - recv4[...].astype(jnp.float32)
 
-    got(3, "sib_x", "sib_l", "sib_r", "sib_o")
-    c3(3)
+    @pl.when(home)
+    def _():
+        got(3, *others)
+        stay(3)
+
+    for copy in copies.values():
+        copy.wait_send()
 
     @pl.when(has_leader)
     def _():
@@ -340,19 +373,13 @@
 
     @pl.when(guest)
     def _():
+        for m in range(4):
+            guest_copy(m).wait_send()
+        ret4.wait_send()
         for i in range(4):
             ret13[i].wait_recv()
             block_ref[0, :, theirs[i]] = keptv[:, theirs[i]] - recv13[:ROWS, theirs[i]].astype(jnp.float32)
             coup_ref[0, :, theirs[i]] = -recv13[ROWS:, theirs[i]].astype(jnp.float32)
-
-    for copy in copies.values():
-        copy.wait_send()
-
-    @pl.when(guest)
-    def _():
-        for m in range(4):
-            guest_copy(m).wait_send()
-        ret4.wait_send()
         for i in range(4):
             ret13[i].wait_send()
 

time: 49 us -> 48.4 us (0.988)
  no operation moved by 1% of the time
where the time goes in v5:
time: 48.4 us; the launch traced here: 48.1 us
  Pallas kernels  47.5 us (98%)
  between operations  0.64 us (1%)
    pallas_call x1, Pallas kernels, body(): pl.pallas_call(kernel, out_shape=shapes, in_specs=[pl.BlockSpec(memory_sp...  46.6 us

profile of v5, /device:TPU:1, one launch (start us, length us, event | category | flops | bytes accessed | tf_op | source)
XLA Modules:
  0.0 48.1 jit_solution(3788635574439448275)
XLA Ops:
  0.6 46.6 %shard_map.94 = (f32[1,64,1024]{2,1,0:T(8,128)S(1)}, f32[1,64,1024]{2,1,0:T(8,128)S(1)}, f32[1,64,1024]{2,1,0:T(8,128)S(1)}) custom-call(f32[1,64,1024]{2,1,0:T(8,128)} %kept_ref.1, bf16[1,64,1024]{2,1,0:T(8,128)(2,1)} %bitcast.1, bf16[1,64,1024]{2,1,0:T(8,128)(2,1)} %cout_ref.1, bf16[1,64,1024]{2,1,0:T(8,128)(2,1)} %w_ref.1, bf16[1,64,1024]{2,1,0:T(8,128)(2,1)} %sk_ref.1, ...), custom_call_target="tpu_custom_call" | custom-call | tf_op jit(solution)/shard_map/pallas_call | solution.py:409
  47.2 0.9 %shard_map.95 = (f32[1,64,1024]{2,1,0:T(8,128)}, f32[1,64,1024]{2,1,0:T(8,128)}, f32[1,64,1024]{2,1,0:T(8,128)}) custom-call(f32[1,64,1024]{2,1,0:T(8,128)S(1)} %get-tuple-element.6.refs_0_, f32[1,64,1024]{2,1,0:T(8,128)S(1)} %get-tuple-element.7.refs_1_, f32[1,64,1024]{2,1,0:T(8,128)S(1)} %get-tuple-element.8.refs_2_), custom_call_target="tpu_custom_call" | custom-call | tf_op jit(solution)/shard_map/pallas_call | solution.py:425

commit v6 on v5

--- a/solution.py
+++ b/solution.py
@@ -16,9 +16,9 @@
 )
 NKEYS = len(KEYS)
 SWAP0 = 4 * NKEYS
-RET0 = SWAP0 + 4
+RET0 = SWAP0 + 5
 NSEM = RET0 + 10
-SPLIT = ((32, 16, 16),) * 4
+SPLIT = ((32, 16, 16), (32, 16, 16), (32, 16, 16), (16, 16, 16))
 
 
 SEQ = (('s1', 0), ('s1', 1), ('s1', 2), ('o2', 0), ('s2', 0), ('s1', 3), ('o2', 1), ('s2', 1), ('s3', 0), ('o2', 2), ('s2', 2), ('s3', 1), ('s4a', 0), ('s4b', 0), ('o2', 3), ('s2', 3), ('c0', 0), ('c0', 1), ('s3', 2), ('s4a', 1), ('s4b', 1), ('c1', 0), ('c1', 1), ('s3', 3), ('s4a', 2), ('s4b', 2), ('c2', 0), ('c2', 1))
@@ -93,12 +93,18 @@
     def home_copy(m):
         return pltpu.make_async_copy(own[m], rows(m, panel, 0, ROWS), lsem.at[3 + m])
 
-    def guest_copy(m):
-        return pltpu.make_async_remote_copy(
-            src_ref=own[m], dst_ref=rows(m, panel, 0, ROWS),
-            send_sem=ssem.at[SWAP0 + m], recv_sem=rsem.at[SWAP0 + m],
-            device_id=partner, device_id_type=MESH,
-        )
+    def guest_copies(m):
+        a = SPLIT[0][0] if m == 0 else ROWS
+        pieces = ((0, a, SWAP0 + m), (a, ROWS - a, SWAP0 + 4))
+        return [
+            pltpu.make_async_remote_copy(
+                src_ref=own[m].at[pl.ds(r0, n)], dst_ref=rows(m, panel, r0, n),
+                send_sem=ssem.at[at], recv_sem=rsem.at[at],
+                device_id=partner, device_id_type=MESH,
+            )
+            for r0, n, at in pieces
+            if n
+        ]
 
     @pl.when(home)
     def _():
@@ -119,20 +125,25 @@
     @pl.when(guest)
     def _():
         for m in range(4):
-            guest_copy(m).start()
+            for copy in guest_copies(m):
+                copy.start()
 
     @pl.when(has_leader)
     def _():
         pl.semaphore_signal(ready, inc=1, device_id=leader, device_id_type=MESH)
 
-    def swapped(m):
-        @pl.when(home)
-        def _():
-            home_copy(m).wait()
-
-        @pl.when(guest)
-        def _():
-            guest_copy(m).wait_recv()
+    def swapped(m, i=0):
+        if i == 0:
+
+            @pl.when(home)
+            def _():
+                home_copy(m).wait()
+
+        if i < len(guest_copies(m)):
+
+            @pl.when(guest)
+            def _():
+                guest_copies(m)[i].wait_recv()
 
     copies = {}
 
@@ -162,6 +173,7 @@
         swapped(m)
         send(m, "a_R", mine, 0, a, right)
         send(m, "a_L", mine, 0, a, left)
+        swapped(m, 1)
         send(m, "b_Y", mine, a, ROWS - a, across)
 
     def o2(m):
@@ -374,7 +386,8 @@
     @pl.when(guest)
     def _():
         for m in range(4):
-            guest_copy(m).wait_send()
+            for copy in guest_copies(m):
+                copy.wait_send()
         ret4.wait_send()
         for i in range(4):
             ret13[i].wait_recv()

time: 48.4 us -> 47.6 us (0.983)
  Pallas kernels: 47.5 us -> 46.9 us
    pallas_call x1, Pallas kernels: 46.6 us -> 46 us  [body(): pl.pallas_call(kernel, out_shape=shapes, in_specs=[pl.BlockSpec(memory_sp...]
where the time goes in v6:
time: 47.6 us; the launch traced here: 47.5 us
  Pallas kernels  46.9 us (99%)
  between operations  0.64 us (1%)
    pallas_call x1, Pallas kernels, body(): pl.pallas_call(kernel, out_shape=shapes, in_specs=[pl.BlockSpec(memory_sp...  46 us

profile of v6, /device:TPU:1, one launch (start us, length us, event | category | flops | bytes accessed | tf_op | source)
XLA Modules:
  0.0 47.5 jit_solution(15945524945221951292)
XLA Ops:
  0.6 46.0 %shard_map.94 = (f32[1,64,1024]{2,1,0:T(8,128)S(1)}, f32[1,64,1024]{2,1,0:T(8,128)S(1)}, f32[1,64,1024]{2,1,0:T(8,128)S(1)}) custom-call(f32[1,64,1024]{2,1,0:T(8,128)} %kept_ref.1, bf16[1,64,1024]{2,1,0:T(8,128)(2,1)} %bitcast.1, bf16[1,64,1024]{2,1,0:T(8,128)(2,1)} %cout_ref.1, bf16[1,64,1024]{2,1,0:T(8,128)(2,1)} %w_ref.1, bf16[1,64,1024]{2,1,0:T(8,128)(2,1)} %sk_ref.1, ...), custom_call_target="tpu_custom_call" | custom-call | tf_op jit(solution)/shard_map/pallas_call | solution.py:422
  46.6 0.9 %shard_map.95 = (f32[1,64,1024]{2,1,0:T(8,128)}, f32[1,64,1024]{2,1,0:T(8,128)}, f32[1,64,1024]{2,1,0:T(8,128)}) custom-call(f32[1,64,1024]{2,1,0:T(8,128)S(1)} %get-tuple-element.6.refs_0_, f32[1,64,1024]{2,1,0:T(8,128)S(1)} %get-tuple-element.7.refs_1_, f32[1,64,1024]{2,1,0:T(8,128)S(1)} %get-tuple-element.8.refs_2_), custom_call_target="tpu_custom_call" | custom-call | tf_op jit(solution)/shard_map/pallas_call | solution.py:438

commit v7 on v6

--- a/solution.py
+++ b/solution.py
@@ -21,7 +21,7 @@
 SPLIT = ((32, 16, 16), (32, 16, 16), (32, 16, 16), (16, 16, 16))
 
 
-SEQ = (('s1', 0), ('s1', 1), ('s1', 2), ('o2', 0), ('s2', 0), ('s1', 3), ('o2', 1), ('s2', 1), ('s3', 0), ('o2', 2), ('s2', 2), ('s3', 1), ('s4a', 0), ('s4b', 0), ('o2', 3), ('s2', 3), ('c0', 0), ('c0', 1), ('s3', 2), ('s4a', 1), ('s4b', 1), ('c1', 0), ('c1', 1), ('s3', 3), ('s4a', 2), ('s4b', 2), ('c2', 0), ('c2', 1))
+SEQ = (('s1', 0), ('s1', 1), ('s1', 2), ('o2', 0), ('s2', 0), ('s1', 3), ('o2', 1), ('s2', 1), ('s3', 0), ('o2', 2), ('s2', 2), ('s3', 1), ('o2', 3), ('s2', 3), ('s4a', 0), ('s4b', 0), ('c0', 0), ('c0', 1), ('s3', 2), ('s4a', 1), ('s4b', 1), ('c1', 0), ('c1', 1), ('s3', 3), ('s4a', 2), ('s4b', 2), ('c2', 0), ('c2', 1))
 
 
 def nt(left, right):

time: 47.6 us -> 47.2 us (level)
  Pallas kernels: 46.9 us -> 46.3 us
    pallas_call x1, Pallas kernels: 46 us -> 45.4 us  [body(): pl.pallas_call(kernel, out_shape=shapes, in_specs=[pl.BlockSpec(memory_sp...]
where the time goes in v7:
time: 47.2 us; the launch traced here: 47 us
  Pallas kernels  46.3 us (98%)
  between operations  0.64 us (1%)
    pallas_call x1, Pallas kernels, body(): pl.pallas_call(kernel, out_shape=shapes, in_specs=[pl.BlockSpec(memory_sp...  45.4 us

profile of v7, /device:TPU:1, one launch (start us, length us, event | category | flops | bytes accessed | tf_op | source)
XLA Modules:
  0.0 47.0 jit_solution(13658830113055168918)
XLA Ops:
  0.6 45.4 %shard_map.94 = (f32[1,64,1024]{2,1,0:T(8,128)S(1)}, f32[1,64,1024]{2,1,0:T(8,128)S(1)}, f32[1,64,1024]{2,1,0:T(8,128)S(1)}) custom-call(f32[1,64,1024]{2,1,0:T(8,128)} %kept_ref.1, bf16[1,64,1024]{2,1,0:T(8,128)(2,1)} %bitcast.1, bf16[1,64,1024]{2,1,0:T(8,128)(2,1)} %cout_ref.1, bf16[1,64,1024]{2,1,0:T(8,128)(2,1)} %w_ref.1, bf16[1,64,1024]{2,1,0:T(8,128)(2,1)} %sk_ref.1, ...), custom_call_target="tpu_custom_call" | custom-call | tf_op jit(solution)/shard_map/pallas_call | solution.py:422
  46.1 0.9 %shard_map.95 = (f32[1,64,1024]{2,1,0:T(8,128)}, f32[1,64,1024]{2,1,0:T(8,128)}, f32[1,64,1024]{2,1,0:T(8,128)}) custom-call(f32[1,64,1024]{2,1,0:T(8,128)S(1)} %get-tuple-element.6.refs_0_, f32[1,64,1024]{2,1,0:T(8,128)S(1)} %get-tuple-element.7.refs_1_, f32[1,64,1024]{2,1,0:T(8,128)S(1)} %get-tuple-element.8.refs_2_), custom_call_target="tpu_custom_call" | custom-call | tf_op jit(solution)/shard_map/pallas_call | solution.py:438

commit v8 on v7

--- a/solution.py
+++ b/solution.py
@@ -21,7 +21,7 @@
 SPLIT = ((32, 16, 16), (32, 16, 16), (32, 16, 16), (16, 16, 16))
 
 
-SEQ = (('s1', 0), ('s1', 1), ('s1', 2), ('o2', 0), ('s2', 0), ('s1', 3), ('o2', 1), ('s2', 1), ('s3', 0), ('o2', 2), ('s2', 2), ('s3', 1), ('o2', 3), ('s2', 3), ('s4a', 0), ('s4b', 0), ('c0', 0), ('c0', 1), ('s3', 2), ('s4a', 1), ('s4b', 1), ('c1', 0), ('c1', 1), ('s3', 3), ('s4a', 2), ('s4b', 2), ('c2', 0), ('c2', 1))
+SEQ = (('s1', 0), ('s1', 1), ('s1', 2), ('o2', 0), ('s2', 0), ('s1', 3), ('o2', 1), ('s2', 1), ('s3', 0), ('o2', 2), ('s2', 2), ('o2', 3), ('s3', 1), ('s2', 3), ('s4a', 0), ('s4b', 0), ('c0', 0), ('c0', 1), ('s3', 2), ('s4a', 1), ('s4b', 1), ('c1', 0), ('c1', 1), ('s3', 3), ('s4a', 2), ('s4b', 2), ('c2', 0), ('c2', 1))
 
 
 def nt(left, right):

time: 47.2 us -> 47.8 us (1.013)
  Pallas kernels: 46.3 us -> 47 us
    pallas_call x1, Pallas kernels: 45.4 us -> 46.1 us  [body(): pl.pallas_call(kernel, out_shape=shapes, in_specs=[pl.BlockSpec(memory_sp...]
where the time goes in v8:
time: 47.8 us; the launch traced here: 47.7 us
  Pallas kernels  47 us (98%)
  between operations  0.64 us (1%)
    pallas_call x1, Pallas kernels, body(): pl.pallas_call(kernel, out_shape=shapes, in_specs=[pl.BlockSpec(memory_sp...  46.1 us

profile of v8, /device:TPU:1, one launch (start us, length us, event | category | flops | bytes accessed | tf_op | source)
XLA Modules:
  0.0 47.7 jit_solution(5364562841020365178)
XLA Ops:
  0.6 46.1 %shard_map.94 = (f32[1,64,1024]{2,1,0:T(8,128)S(1)}, f32[1,64,1024]{2,1,0:T(8,128)S(1)}, f32[1,64,1024]{2,1,0:T(8,128)S(1)}) custom-call(f32[1,64,1024]{2,1,0:T(8,128)} %kept_ref.1, bf16[1,64,1024]{2,1,0:T(8,128)(2,1)} %bitcast.1, bf16[1,64,1024]{2,1,0:T(8,128)(2,1)} %cout_ref.1, bf16[1,64,1024]{2,1,0:T(8,128)(2,1)} %w_ref.1, bf16[1,64,1024]{2,1,0:T(8,128)(2,1)} %sk_ref.1, ...), custom_call_target="tpu_custom_call" | custom-call | tf_op jit(solution)/shard_map/pallas_call | solution.py:422
  46.8 0.9 %shard_map.95 = (f32[1,64,1024]{2,1,0:T(8,128)}, f32[1,64,1024]{2,1,0:T(8,128)}, f32[1,64,1024]{2,1,0:T(8,128)}) custom-call(f32[1,64,1024]{2,1,0:T(8,128)S(1)} %get-tuple-element.6.refs_0_, f32[1,64,1024]{2,1,0:T(8,128)S(1)} %get-tuple-element.7.refs_1_, f32[1,64,1024]{2,1,0:T(8,128)S(1)} %get-tuple-element.8.refs_2_), custom_call_target="tpu_custom_call" | custom-call | tf_op jit(solution)/shard_map/pallas_call | solution.py:438
